TPU v7x, 256 devices: a whole 4x4x8 slice. The times are simulated.
256 devices in a mesh: prow: 32 (over z, x), pcol: 8 (over y, core).
Axes of the slice: x: 4, y: 4, z: 8, core: 2. Of those that a mesh axis runs over, the one named last changes fastest.
Arguments:
- matrix: float32 [16384, 24576], P('prow', 'pcol'), may hold values from -3 to 3
- pivots: int32 [256], replicated, may hold values from 128 to 16383, as said below
- lower_inverse: float32 [2, 128, 128], replicated, may hold values from -0.5 to 0.5
- upper_inverse: float32 [2, 128, 128], replicated, may hold values from -0.09375 to 0.09375
Outputs:
- factored: float32 [16384, 24576], P('prow', 'pcol')
Inputs may be any that keep to these rules, and one draw needn't show every extreme that they name: For each section t, the entries pivots[t * 128] to pivots[(t + 1) * 128 - 1] are distinct and lie between (t + 1) * 128 and 16383.
All inputs are finite; a program needn't handle non-finite values.
Results may differ from a plain program's by a relative error of at most 0.0003.
Values sent between devices are 32-bit elements; how exact they have to be, the bound alone decides.
A program may use at most 64 MiB of HBM per device.

v0:
```python
import jax
import jax.numpy as jnp
from jax import lax
from jax.sharding import PartitionSpec as P


def broadcast(block, axis, holder):
    block = jnp.where(lax.axis_index(axis) == holder, block, jnp.zeros_like(block))
    return lax.psum(block, axis)


def shards(matrix, pivots, lower_inverse, upper_inverse):
    process_row = lax.axis_index("prow")
    process_col = lax.axis_index("pcol")
    prow_count = lax.axis_size("prow")
    pcol_count = lax.axis_size("pcol")
    rows_dev, cols_dev = matrix.shape
    block = lower_inverse.shape[1]
    row_offsets = jnp.arange(rows_dev, dtype=jnp.int32)
    glob_rows = (row_offsets // block * prow_count + process_row) * block + row_offsets % block
    col_offsets = jnp.arange(cols_dev, dtype=jnp.int32)
    glob_cols = (col_offsets // block * pcol_count + process_col) * block + col_offsets % block
    block_ids = jnp.arange(block, dtype=jnp.int32)
    current = matrix
    for section in range(2):
        wanted = jnp.concatenate(
            [section * block + block_ids, pivots[section * block : (section + 1) * block]]
        )
        owner_row = wanted // block % prow_count
        local_row = wanted // block // prow_count * block + wanted % block
        owned = owner_row == process_row
        picked = jnp.where(owned[:, None], current[local_row], 0.0)
        in_play = lax.psum(picked, "prow")
        arrived = jnp.concatenate([in_play[block:], in_play[:block]], axis=0)
        current = current.at[jnp.where(owned, local_row, rows_dev)].set(arrived, mode="drop")
        lower_unit = jnp.tril(lower_inverse[section], -1) + jnp.eye(block, dtype=jnp.float32)
        upper_tri = jnp.triu(upper_inverse[section])
        upper_rows = jnp.dot(lower_unit, arrived[:block], precision=lax.Precision.HIGHEST)
        panel_block = current[:, :block]
        solved = jnp.dot(panel_block, upper_tri, precision=lax.Precision.HIGHEST)
        panel = broadcast(solved, "pcol", section)
        beneath = glob_rows >= (section + 1) * block
        rightward = glob_cols >= (section + 1) * block
        updated = current - jnp.dot(panel, upper_rows, precision=lax.Precision.HIGHEST)
        current = jnp.where(beneath[:, None] & rightward[None, :], updated, current)
        panel_owner = process_col == section
        current = current.at[:, :block].set(
            jnp.where(beneath[:, None] & panel_owner, panel, current[:, :block])
        )
        block_owner = process_row == section
        current = current.at[:block].set(
            jnp.where(block_owner & rightward[None, :], upper_rows, current[:block])
        )
    return current


def solution(mesh):
    placed = (P("prow", "pcol"), P(), P(), P())
    return jax.shard_map(
        shards, mesh=mesh, in_specs=placed, out_specs=P("prow", "pcol"), check_vma=False
    )
```

profile of v0, /device:TPU:17, one launch (start us, length us, event | category | flops | bytes accessed | tf_op | source)
XLA Modules:
  0.0 529.4 jit_solution(18110700192669430466)
XLA Ops:
  6.5 6.2 %copy.16 = f32[512,3072]{1,0:T(8,128)} copy(f32[512,3072]{1,0:T(8,128)} %param.12) | data formatting | bytes 12582912
  12.8 6.0 %gather_fusion = f32[256,3072]{1,0:T(8,128)S(1)} fusion(f32[512,3072]{1,0:T(8,128)} %copy.16, s32[1024]{0:T(1024)S(1)} %pad_clamp_fusion.1), kind=kCustom, calls=%fused_computation | custom fusion | bytes 6292480 | tf_op jit(solution)/shard_map/gather | solution.py:32
  18.9 2.1 broadcast_select_fusion.1
  21.8 156.5 %all-reduce.5.cloned.1.call-done = f32[256,3072]{1,0:T(8,128)} async-done(((f32[256,3072]{1,0:T(8,128)}), f32[256,3072]{1,0:T(8,128)}) %all-reduce.5.cloned.1.call-update) | async-done | bytes 3145744 | tf_op jit(solution)/shard_map/psum | solution.py:33
  178.3 2.1 fusion.66
  180.5 8.0 %scatter_custom_fusion = f32[512,3072]{1,0:T(8,128)} fusion(f32[512,3072]{1,0:T(8,128)} %copy.16, s32[256]{0:T(256)S(1)} %bitcast.34, f32[128,3072]{1,0:T(8,128)S(1)} %get-tuple-element.62, f32[]{:T(128)} %constant.263, f32[128,3072]{1,0:T(8,128)S(1)} %get-tuple-element.61), kind=kCustom, calls=%fused_computation.6 | custom fusion | flops 786432 | bytes 9437696 | tf_op jit(solution)/shard_map/scatter | solution.py:35
  188.5 2.1 convolution_select_fusion.1
  190.8 2.9 fusion.14
  193.7 59.5 %all-reduce.7.cloned.1.call-done = f32[512,128]{1,0:T(8,128)} async-done(((f32[512,128]{1,0:T(8,128)}), f32[512,128]{1,0:T(8,128)}) %all-reduce.7.cloned.1.call-update) | async-done | bytes 262160 | tf_op jit(solution)/shard_map/psum | solution.py:9
  253.3 10.1 %subtract_select_fusion.1 = f32[512,3072]{1,0:T(8,128)} fusion(f32[512,3072]{1,0:T(8,128)} %scatter_custom_fusion, f32[512,128]{1,0:T(8,128)} %all-reduce.7.cloned.1.call-done, f32[128,3072]{1,0:T(8,128)S(1)} %fusion.14, pred[3072]{0:T(1024)(128)(4,1)S(1)} %get-tuple-element.70, pred[512]{0:T(512)(128)(4,1)S(1)} %get-tuple-element.68), kind=kOutput, calls=%fused_computation.5 | convolution fusion | flops 2420637696 | bytes 14421504 | tf_op jit(solution)/shard_map/dot_general | solution.py:44
  263.4 2.4 fusion.10
  265.8 2.7 fusion.9
  268.5 6.0 %gather_fusion.1 = f32[256,3072]{1,0:T(8,128)S(1)} fusion(f32[512,3072]{1,0:T(8,128)} %fusion.9, s32[1024]{0:T(1024)S(1)} %pad_clamp_fusion), kind=kCustom, calls=%fused_computation.1 | custom fusion | bytes 6292480 | tf_op jit(solution)/shard_map/gather | solution.py:32
  274.5 2.1 broadcast_select_fusion
  276.8 156.5 %all-reduce.9.cloned.1.call-done = f32[256,3072]{1,0:T(8,128)} async-done(((f32[256,3072]{1,0:T(8,128)}), f32[256,3072]{1,0:T(8,128)}) %all-reduce.9.cloned.1.call-update) | async-done | bytes 3145744 | tf_op jit(solution)/shard_map/psum | solution.py:33
  433.3 2.1 fusion.65
  435.4 8.0 %scatter_custom_fusion.1 = f32[512,3072]{1,0:T(8,128)} fusion(f32[512,3072]{1,0:T(8,128)} %fusion.9, s32[256]{0:T(256)S(1)} %bitcast.35, f32[128,3072]{1,0:T(8,128)S(1)} %get-tuple-element.60, f32[]{:T(128)} %constant.263, f32[128,3072]{1,0:T(8,128)S(1)} %get-tuple-element.59), kind=kCustom, calls=%fused_computation.10 | custom fusion | flops 786432 | bytes 9437696 | tf_op jit(solution)/shard_map/scatter | solution.py:35
  443.4 2.1 convolution_select_fusion
  445.5 2.9 fusion.15
  448.4 59.8 %all-reduce.11.cloned.1.call-done = f32[512,128]{1,0:T(8,128)} async-done(((f32[512,128]{1,0:T(8,128)}), f32[512,128]{1,0:T(8,128)}) %all-reduce.11.cloned.1.call-update) | async-done | bytes 262160 | tf_op jit(solution)/shard_map/psum | solution.py:9
  508.2 8.5 %subtract_select_fusion = f32[512,3072]{1,0:T(8,128)S(1)} fusion(f32[512,3072]{1,0:T(8,128)} %scatter_custom_fusion.1, f32[512,128]{1,0:T(8,128)} %all-reduce.11.cloned.1.call-done, f32[128,3072]{1,0:T(8,128)S(1)} %fusion.15, pred[3072]{0:T(1024)(128)(4,1)S(1)} %broadcast_compare_fusion, pred[512]{0:T(512)(128)(4,1)S(1)} %broadcast_compare_fusion.2), kind=kOutput, calls=%fused_computation.4 | convolution fusion | flops 2420637696 | bytes 14421504 | tf_op jit(solution)/shard_map/dot_general | solution.py:44
  516.7 0.8 fusion.11
  517.5 2.7 copy-done
  520.2 2.7 fusion.8
  (39 shorter events, 1.3 us)
Async XLA Ops:
  6.5 6.3 %copy-start.5 = (s32[256]{0:T(256)S(1)}, s32[256]{0:T(256)}, u32[]{:S(2)}) copy-start(s32[256]{0:T(256)} %param.13) | copy-start | bytes 3076
  6.5 171.8 %all-reduce.5.cloned.1.call-start = ((), (), s32[]{:S(2)}) async-start(), calls=%async_computation | async-start | bytes 6291456 | tf_op jit(solution)/shard_map/psum | solution.py:33
  21.0 232.3 %all-reduce.7.cloned.1.call-start = ((), (), s32[]{:S(2)}) async-start(), calls=%async_computation.1 | async-start | bytes 524288 | tf_op jit(solution)/shard_map/psum | solution.py:9
  180.4 8.1 %copy-start.3 = (f32[2,128,128]{2,1,0:T(8,128)S(1)}, f32[2,128,128]{2,1,0:T(8,128)}, u32[]{:S(2)}) copy-start(f32[2,128,128]{2,1,0:T(8,128)} %param.15) | copy-start | bytes 393220
  180.4 10.4 %copy-start.4 = (f32[2,128,128]{2,1,0:T(8,128)S(1)}, f32[2,128,128]{2,1,0:T(8,128)}, u32[]{:S(2)}) copy-start(f32[2,128,128]{2,1,0:T(8,128)} %param.14) | copy-start | bytes 393220
  190.6 242.7 %all-reduce.9.cloned.1.call-start = ((), (), s32[]{:S(2)}) async-start(), calls=%async_computation.2 | async-start | bytes 6291456 | tf_op jit(solution)/shard_map/psum | solution.py:33
  253.3 10.1 %copy-start.1 = (f32[512,128]{1,0:T(8,128)S(1)}, f32[512,128]{1,0:T(8,128)}, u32[]{:S(2)}) copy-start(f32[512,128]{1,0:T(8,128)} %all-reduce.7.cloned.1.call-done) | copy-start | bytes 786436
  276.6 231.6 %all-reduce.11.cloned.1.call-start = ((), (), s32[]{:S(2)}) async-start(), calls=%async_computation.3 | async-start | bytes 524288 | tf_op jit(solution)/shard_map/psum | solution.py:9
  508.2 8.5 %copy-start.2 = (f32[512,128]{1,0:T(8,128)S(1)}, f32[512,128]{1,0:T(8,128)}, u32[]{:S(2)}) copy-start(f32[512,128]{1,0:T(8,128)} %all-reduce.11.cloned.1.call-done) | copy-start | bytes 786436
  517.5 2.7 copy-start
Sparse Core Ops, SparseCore 0:
  21.1 157.2 all-reduce.4
  190.7 62.5 all-reduce.6
  276.7 156.5 all-reduce.8
  445.6 62.4 all-reduce.10
where the time goes:
time: 533 us; the launch traced here: 529 us
  waiting for transfers between devices  432 us (81%)
  other arithmetic  29.7 us (6%)
  matrix products  28.5 us (5%)
  local copies, waits for them, and re-layouts  25.1 us (5%)
  between operations  13.3 us (2%)
    psum x2, waiting for transfers between devices, shards(): in_play = lax.psum(picked, 'prow')  313 us
    psum x2, waiting for transfers between devices, broadcast(): return lax.psum(block, axis)  119 us
    dot_general x2, matrix products, shards(): jnp.dot(panel, upper_rows, precision=lax.Precision.HIGHEST)  18.6 us
    scatter x2, other arithmetic, shards(): current.at[jnp.where(owned, local_row, rows_dev)].set(arrived, mode='drop')  16.1 us
    gather x2, local copies, waits for them, and re-layouts, shards(): picked = jnp.where(owned[:, None], current[local_row], 0.0)  12 us
  transfers between devices with their start and end apart: 4, of which 4 were waited for; matrix products, arithmetic and copies ran while one was open for 1% of the time, Pallas kernels for 0%

commit v1 on v0

--- a/solution.py
+++ b/solution.py
@@ -1,7 +1,477 @@
+import functools
+
 import jax
 import jax.numpy as jnp
 from jax import lax
+from jax.experimental import pallas as pl
+from jax.experimental.pallas import tpu as pltpu
 from jax.sharding import PartitionSpec as P
+
+MESH = pl.DeviceIdType.MESH
+NB = 128
+ROWS = 512
+COLS = 3072
+NPROW = 32
+REACH_R = 3
+REACH_T = 5
+GROUPS_R = 2 * REACH_R + 1
+GROUPS_T = 2 * REACH_T + 1
+TROWS = 8 * GROUPS_T
+EXT = ROWS + 256 + TROWS
+F32 = jnp.float32
+BF16 = jnp.bfloat16
+
+
+def hp(a, b):
+    return jnp.dot(a, b, precision=lax.Precision.HIGHEST, preferred_element_type=F32)
+
+
+def owner_of(row):
+    return (row // NB) % NPROW
+
+
+def local_of(row):
+    return row // (NB * NPROW) * NB + row % NB
+
+
+def wrapped(distance):
+    return (distance + 16) % NPROW - 16
+
+
+def ranks(key):
+    return jnp.sum((key[None, :] < key[:, None]).astype(jnp.int32), axis=1)
+
+
+def plan(pivots, p):
+    ids = jnp.arange(NB, dtype=jnp.int32)
+    piv0, piv1 = pivots[:NB], pivots[NB:]
+    same = piv1[:, None] == piv0[None, :]
+    onto = piv0[:, None] - NB == ids[None, :]
+    src1 = jnp.where(same.any(1), jnp.sum(jnp.where(same, ids[None, :], 0), 1), piv1)
+    src = jnp.concatenate([piv0, src1])
+    via = jnp.sum(jnp.where(onto, piv1[None, :], 0), 1)
+    dest0 = jnp.where(piv0 < 2 * NB, via, jnp.where(same.any(0), -1, piv0))
+    dest1 = jnp.where(onto.any(0), -1, piv1)
+
+    own, local = owner_of(src), local_of(src)
+    rank = ranks(own * 256 + jnp.arange(256, dtype=jnp.int32))
+    skew = 16 * own + 7 - 2 * rank
+    slot = (rank + (jnp.max(skew) + jnp.min(skew)) // 4) % 256
+    fits = jnp.all(jnp.abs(wrapped(slot // 8 - own)) <= REACH_R)
+    wanted = (8 * (p - REACH_R) + jnp.arange(8 * GROUPS_R, dtype=jnp.int32)) % 256
+    mine = (slot[None, :] == wanted[:, None]) & (own == p)[None, :]
+    index = jnp.sum(jnp.where(mine, local[None, :] + 1, 0), 1) - 1
+    slot_hot = (slot[:, None] == jnp.arange(256)[None, :]).astype(F32)
+
+    row_hots, group_hots, orders = [], [], []
+    for section, dest in enumerate((dest0, dest1)):
+        moves = dest >= 0
+        to = jnp.where(moves, owner_of(dest), ids // 4)
+        rank = ranks(to * NB + ids)
+        skew = 8 * to + 3 - 2 * rank
+        place = (rank + (jnp.max(skew) + jnp.min(skew)) // 4) % NB
+        group = place // 8
+        home = group // 2 * 4 + jnp.where(group % 2 == 0, section, 3 - section)
+        fits = fits & jnp.all((jnp.abs(wrapped(to - home)) <= REACH_T) | ~moves)
+        column = (home - p + REACH_T) % NPROW * 8 + place % 8
+        here = moves & (to == p)
+        row_hots.append(hot((local_of(dest)[None, :] == jnp.arange(ROWS)[:, None]) & here[None, :]))
+        group_hots.append(hot(column[:, None] == jnp.arange(TROWS)[None, :]))
+        orders.append((place[None, :] == ids[:, None]).astype(F32))
+    put = jnp.dot(jnp.concatenate(row_hots, 1), jnp.concatenate(group_hots, 0), preferred_element_type=F32)
+    order = jnp.where(p == 0, orders[0], orders[1])
+    return fits, index, order, slot_hot, put
+
+
+def hot(mask):
+    return mask.astype(BF16)
+
+
+A_CHUNKS = ((0, 128, 1), (128, 512, -1), (640, 640, 1))
+B_CHUNKS = ((1280, 896, 1), (2176, 896, -1))
+SHIFTS = ((0, 128), (1280, 1792), (128, 1152))
+T_CHUNKS = ((0, 128), (128, 2944))
+COPIES = 224
+
+
+def hops(long, way):
+    return 4 if long == way else 3
+
+
+def gather_kernel(index_ref, order_ref, a_hbm, r_ref, t_ref, e_ref, a_ref, pack, inbox, t_pack, load_sem, send_sem, recv_sem):
+    p, q = lax.axis_index("prow"), lax.axis_index("pcol")
+    z, x = lax.div(p, 4), lax.rem(p, 4)
+    y, core = lax.div(q, 2), lax.rem(q, 2)
+    source = p < 2
+    sends, receipts = {}, {}
+    pending = []
+
+    def number(numbers, tag):
+        assert len(numbers) < COPIES or tag in numbers
+        return numbers.setdefault(tag, len(numbers))
+
+    def copy(src, dst, tag, device, recv_tag=None):
+        return pltpu.make_async_remote_copy(
+            src_ref=src,
+            dst_ref=dst,
+            send_sem=send_sem.at[number(sends, tag)],
+            recv_sem=recv_sem.at[number(receipts, recv_tag or tag)],
+            device_id=device,
+            device_id_type=MESH,
+        )
+
+    def send(src, dst, tag, device):
+        c = copy(src, dst, tag, device)
+        c.start()
+        pending.append(c)
+
+    def arrived(dst, tag):
+        copy(dst, dst, tag, core_peer).wait_recv()
+
+    def along(step):
+        return lax.rem(p + step + NPROW, NPROW), q
+
+    def at_z(step):
+        return lax.rem(z + step + 8, 8) * 4 + x, q
+
+    def at_x(step):
+        return z * 4 + lax.rem(x + step + 4, 4), q
+
+    core_peer = (p, y * 2 + 1 - core)
+
+    def block(zz, xx, cols):
+        start = pl.multiple_of((lax.rem(z + zz + 8, 8) * 4 + lax.rem(x + xx + 4, 4)) * 8, 8)
+        return r_ref.at[pl.ds(start, 8), pl.ds(cols[0], cols[1])]
+
+    def plane(zz, cols):
+        start = pl.multiple_of(lax.rem(z + zz + 8, 8) * 32, 32)
+        return r_ref.at[pl.ds(start, 32), pl.ds(cols[0], cols[1])]
+
+    load = pltpu.make_async_copy(a_hbm, a_ref, load_sem.at[0])
+    load.start()
+
+    barrier = pltpu.get_barrier_semaphore()
+
+    def greet(device):
+        pl.semaphore_signal(barrier, inc=1, device_id=device, device_id_type=MESH)
+
+    for step in range(-REACH_T, REACH_T + 1):
+        if step:
+            greet(along(step))
+    greet(core_peer)
+
+    @pl.when(y > 0)
+    def _():
+        greet((p, core))
+
+    from_row = jnp.where((x == 0) | (x == 3), 0, 1)
+
+    @pl.when(p != from_row)
+    def _():
+        greet((from_row, q))
+
+    load.wait()
+
+    def take(m, carry):
+        r = index_ref[m]
+        row = a_ref[pl.ds(jnp.maximum(r, 0), 1), :]
+        pack[pl.ds(m, 1), :] = jnp.where(r >= 0, row, 0.0)
+        return carry
+
+    lax.fori_loop(0, 8 * GROUPS_R, take, 0)
+    pl.semaphore_wait(barrier, 2 * REACH_T + 1 + jnp.where(y == 0, 3, 0) + jnp.where(source, 15, 0))
+
+    def shift(cols):
+        at = pl.ds(*cols)
+        for d in range(-REACH_R, REACH_R + 1):
+            if d:
+                send(pack.at[pl.ds(8 * (d + REACH_R), 8), at], inbox.at[pl.ds(8 * (REACH_R - d), 8), at], ("shift", cols, d), along(d))
+
+    def settle(cols):
+        at = pl.ds(*cols)
+        for d in range(-REACH_R, REACH_R + 1):
+            if d:
+                arrived(inbox.at[pl.ds(8 * (REACH_R - d), 8), at], ("shift", cols, d))
+        total = pack[8 * REACH_R : 8 * REACH_R + 8, at]
+        for d in range(-REACH_R, REACH_R + 1):
+            if d:
+                total = total + inbox[8 * (REACH_R - d) : 8 * (REACH_R - d) + 8, at]
+        r_ref[pl.ds(pl.multiple_of(p * 8, 8), 8), at] = total
+
+    ext_a = e_ref.at[core, pl.ds(0, ROWS)]
+    ext_rt = e_ref.at[core, pl.ds(ROWS, EXT - ROWS)]
+    far_a = e_ref.at[1 - core, pl.ds(0, ROWS)]
+    far_rt = e_ref.at[1 - core, pl.ds(ROWS, EXT - ROWS)]
+
+    shift(SHIFTS[0])
+
+    @pl.when(y == 0)
+    def _():
+        e_ref[core, :ROWS] = a_ref[:, :NB]
+        for step in (1, 3, 2):
+            copy(ext_a, ext_a, ("ya", step), (p, step * 2 + core), ("ya",)).start()
+
+    shift(SHIFTS[1])
+    shift(SHIFTS[2])
+
+    own_t = pl.ds(8 * REACH_T, 8)
+
+    @pl.when(source)
+    def _():
+        def turn(n, carry):
+            at = pl.ds(pl.multiple_of(n * 512, 512), 512)
+            t_pack[:, at] = hp(order_ref[...], a_ref[:NB, at])
+            return carry
+
+        lax.fori_loop(0, COLS // 512, turn, 0)
+        for cols in T_CHUNKS:
+            at = pl.ds(*cols)
+            for g in range(1, 16):
+                to = g // 2 * 4 + (p if g % 2 == 0 else 3 - p)
+                copy(t_pack.at[pl.ds(8 * g, 8), at], t_ref.at[own_t, at], ("ts", cols, g), (to, q), ("ts", cols)).start()
+        t_ref[own_t, :] = t_pack[:8]
+
+    def spread_x(cols):
+        for dx in (1, 3, 2):
+            send(block(0, 0, cols), block(0, 0, cols), ("a1", cols, dx), at_x(dx))
+
+    def joined_x(cols):
+        for dx in (1, 3, 2):
+            arrived(block(0, -dx, cols), ("a1", cols, dx))
+
+    def pass_plane(cols, s):
+        for way in (1, -1):
+            if s > 0:
+                if s > hops(cols[2], way):
+                    continue
+                arrived(plane(-way * s, cols), ("a2", cols, way, s))
+            if s < hops(cols[2], way):
+                part = plane(-way * s, cols)
+                send(part, part, ("a2", cols, way, s + 1), at_z(way))
+
+    def ways_at(cols, s):
+        return [0] if s == 0 else [-way * s for way in (1, -1) if s <= hops(cols[2], way)]
+
+    def pass_block(cols, s):
+        for way in (1, -1):
+            if s > 0:
+                if s > hops(cols[2], way):
+                    continue
+                arrived(block(-way * s, 0, cols), ("b1", cols, way, s))
+            part = block(-way * s, 0, cols)
+            if s < hops(cols[2], way):
+                send(part, part, ("b1", cols, way, s + 1), at_z(way))
+            if s > 0 or way == 1:
+                for dx in (1, -1):
+                    send(part, part, ("b2", cols, -way * s if s else 0, dx), at_x(dx))
+
+    def relay_x(cols, s):
+        for zz in ways_at(cols, s):
+            for dx in (1, -1):
+                arrived(block(zz, -dx, cols), ("b2", cols, zz, dx))
+                if dx == cols[2]:
+                    part = block(zz, -dx, cols)
+                    send(part, part, ("b3", cols, zz), at_x(dx))
+
+    def end_x(cols, s):
+        for zz in ways_at(cols, s):
+            arrived(block(zz, 2, cols), ("b3", cols, zz))
+
+    def t_ready(cols):
+        at = pl.ds(*cols)
+
+        @pl.when(jnp.logical_not(source))
+        def _():
+            arrived(t_ref.at[own_t, at], ("ts", cols))
+
+        for e in range(-REACH_T, REACH_T + 1):
+            if e:
+                send(t_ref.at[own_t, at], t_ref.at[pl.ds(8 * (REACH_T - e), 8), at], ("th", cols, e), along(e))
+
+    def t_done(cols):
+        at = pl.ds(*cols)
+        for e in range(-REACH_T, REACH_T + 1):
+            if e:
+                arrived(t_ref.at[pl.ds(8 * (REACH_T - e), 8), at], ("th", cols, e))
+
+    first, *rest = A_CHUNKS
+    settle(SHIFTS[0])
+    spread_x(first)
+    settle(SHIFTS[1])
+    for cols in B_CHUNKS:
+        pass_block(cols, 0)
+    settle(SHIFTS[2])
+    for cols in rest:
+        spread_x(cols)
+    joined_x(first)
+    pass_plane(first, 0)
+    t_ready(T_CHUNKS[0])
+    for cols in rest:
+        joined_x(cols)
+        pass_plane(cols, 0)
+    for s in range(1, 5):
+        pass_plane(first, s)
+        for cols in B_CHUNKS:
+            pass_block(cols, s)
+        for cols in rest:
+            pass_plane(cols, s)
+        for cols in B_CHUNKS:
+            relay_x(cols, s - 1)
+        if s == 2:
+            t_ready(T_CHUNKS[1])
+    t_done(T_CHUNKS[0])
+
+    @pl.when(y == 0)
+    def _():
+        e_ref[core, ROWS : ROWS + 256] = r_ref[:, :NB]
+        e_ref[core, ROWS + 256 :] = t_ref[:, :NB]
+        for step in (1, 3, 2):
+            copy(ext_rt, ext_rt, ("yr", step), (p, step * 2 + core), ("yr",)).start()
+
+    @pl.when(y > 0)
+    def _():
+        arrived(ext_a, ("ya",))
+
+    send(ext_a, ext_a, ("ca",), core_peer)
+    for cols in B_CHUNKS:
+        relay_x(cols, 4)
+
+    @pl.when(y > 0)
+    def _():
+        arrived(ext_rt, ("yr",))
+
+    send(ext_rt, ext_rt, ("cr",), core_peer)
+    for s in range(5):
+        for cols in B_CHUNKS:
+            end_x(cols, s)
+    t_done(T_CHUNKS[1])
+    arrived(far_a, ("ca",))
+    arrived(far_rt, ("cr",))
+    for c in pending:
+        c.wait_send()
+
+    @pl.when(y == 0)
+    def _():
+        for step in (1, 3, 2):
+            copy(ext_a, ext_a, ("ya", step), (p, step * 2 + core), ("ya",)).wait_send()
+            copy(ext_rt, ext_rt, ("yr", step), (p, step * 2 + core), ("yr",)).wait_send()
+
+    @pl.when(source)
+    def _():
+        for cols in T_CHUNKS:
+            at = pl.ds(*cols)
+            for g in range(1, 16):
+                to = g // 2 * 4 + (p if g % 2 == 0 else 3 - p)
+                copy(t_pack.at[pl.ds(8 * g, 8), at], t_ref.at[own_t, at], ("ts", cols, g), (to, q), ("ts", cols)).wait_send()
+
+
+def gather(matrix, index, order):
+    vmem = pl.BlockSpec(memory_space=pltpu.VMEM)
+    return pl.pallas_call(
+        gather_kernel,
+        out_shape=[
+            jax.ShapeDtypeStruct((256, COLS), F32),
+            jax.ShapeDtypeStruct((TROWS, COLS), F32),
+            jax.ShapeDtypeStruct((2, EXT, NB), F32),
+        ],
+        in_specs=[pl.BlockSpec(memory_space=pltpu.SMEM), vmem, pl.BlockSpec(memory_space=pl.ANY)],
+        out_specs=[vmem, vmem, vmem],
+        scratch_shapes=[
+            pltpu.VMEM((ROWS, COLS), F32),
+            pltpu.VMEM((8 * GROUPS_R, COLS), F32),
+            pltpu.VMEM((8 * GROUPS_R, COLS), F32),
+            pltpu.VMEM((NB, COLS), F32),
+            pltpu.SemaphoreType.DMA((1,)),
+            pltpu.SemaphoreType.DMA((COPIES,)),
+            pltpu.SemaphoreType.DMA((COPIES,)),
+        ],
+        compiler_params=pltpu.CompilerParams(collective_id=0, has_side_effects=True, vmem_limit_bytes=48 << 20),
+        name="gather_rows",
+    )(index, order, matrix)
+
+
+WIDTH = 512
+
+
+def split(x):
+    high = x.astype(BF16)
+    return high, (x - high.astype(F32)).astype(BF16)
+
+
+def finish_kernel(a_ref, r_ref, t_ref, e_ref, put_ref, slot_ref, low_ref, up_ref, o_ref, w_ref, put16_ref, keep_ref, first_ref):
+    step = pl.program_id(0)
+    p, q = lax.axis_index("prow"), lax.axis_index("pcol")
+
+    @pl.when(step == 0)
+    def _():
+        row = lax.broadcasted_iota(jnp.int32, (NB, NB), 0)
+        col = lax.broadcasted_iota(jnp.int32, (NB, NB), 1)
+        lower = [jnp.where(row > col, low_ref[t], jnp.where(row == col, 1.0, 0.0)) for t in range(2)]
+        upper = [jnp.where(row <= col, up_ref[t], 0.0) for t in range(2)]
+        put = put_ref[...]
+        top = lax.broadcasted_iota(jnp.int32, (ROWS, 1), 0) < NB
+        at0, at1 = top & (p == 0), top & (p == 1)
+        keep = jnp.where(at0 | at1, 0.0, 1.0 - jnp.sum(put, axis=1, keepdims=True))
+        keep_ref[...] = jnp.broadcast_to(keep, (ROWS, NB))
+        put16_ref[...] = put.astype(BF16)
+        pi0, pi1 = slot_ref[:NB], slot_ref[NB:]
+        g0, g1 = hp(lower[0], pi0), hp(lower[1], pi1)
+        r0, r1 = e_ref[0, ROWS : ROWS + 256], e_ref[1, ROWS : ROWS + 256]
+        k0 = hp(r0, upper[0])
+        m1 = g1 - hp(hp(g1, k0), g0)
+        u01 = hp(g0, r1)
+        c0 = keep * e_ref[0, :ROWS] + hp(put, e_ref[0, ROWS + 256 :])
+        c1 = keep * e_ref[1, :ROWS] + hp(put, e_ref[1, ROWS + 256 :])
+        pis = jnp.where(p == 0, pi0, pi1)
+        blank = jnp.zeros((ROWS - NB, NB), F32)
+        c0 = jnp.where(at0 | at1, jnp.concatenate([hp(pis, r0), blank], 0), c0)
+        c1 = jnp.where(at1, jnp.concatenate([hp(pi1, r1), blank], 0), c1)
+        panel0 = hp(c0, upper[0])
+        middle = c1 - hp(panel0, u01)
+        panel1 = hp(middle, upper[1])
+        w = hp(panel0, g0) + hp(panel1, m1)
+        blank2 = jnp.zeros((ROWS - NB, 256), F32)
+        w = jnp.where(at0 | at1, jnp.concatenate([-jnp.where(p == 0, g0, m1), blank2], 0), w)
+        high, low = split(-w)
+        w_ref[:, :256] = high
+        w_ref[:, 256:512] = high
+        w_ref[:, 512:] = low
+        u01_tall = jnp.concatenate([u01, blank], 0)
+        first0 = jnp.where(at0, c0, panel0)
+        first1 = jnp.where(at0, u01_tall, jnp.where(at1, middle, panel1))
+        first_ref[...] = jnp.where(q == 0, first0, first1)
+
+    r_high, r_low = split(r_ref[...])
+    t_high, t_low = split(t_ref[...])
+    dot = functools.partial(jnp.dot, preferred_element_type=F32)
+    rows = jnp.concatenate([r_high, r_low, r_high], 0)
+    put16 = put16_ref[...]
+    moved = dot(put16, t_high) + dot(put16, t_low)
+    o_ref[...] = keep_ref[:, :1] * a_ref[...] + (moved + dot(w_ref[...], rows))
+
+    @pl.when((step == 0) & (q < 2))
+    def _():
+        o_ref[:, :NB] = first_ref[...]
+
+
+def finish(matrix, rows, tops, ext, put, slot_hot, lower_inverse, upper_inverse):
+    whole = lambda *dims: pl.BlockSpec(dims, lambda i: (0,) * len(dims))
+    wide = lambda n: pl.BlockSpec((n, WIDTH), lambda i: (0, i))
+    return pl.pallas_call(
+        finish_kernel,
+        grid=(COLS // WIDTH,),
+        out_shape=jax.ShapeDtypeStruct((ROWS, COLS), F32),
+        in_specs=[wide(ROWS), wide(256), wide(TROWS), whole(2, EXT, NB), whole(ROWS, TROWS), whole(256, 256), whole(2, NB, NB), whole(2, NB, NB)],
+        out_specs=wide(ROWS),
+        scratch_shapes=[
+            pltpu.VMEM((ROWS, 768), BF16),
+            pltpu.VMEM((ROWS, TROWS), BF16),
+            pltpu.VMEM((ROWS, NB), F32),
+            pltpu.VMEM((ROWS, NB), F32),
+        ],
+        compiler_params=pltpu.CompilerParams(vmem_limit_bytes=48 << 20),
+        name="finish",
+    )(matrix, rows, tops, ext, put, slot_hot, lower_inverse, upper_inverse)
 
 
 def broadcast(block, axis, holder):
@@ -9,7 +479,7 @@
     return lax.psum(block, axis)
 
 
-def shards(matrix, pivots, lower_inverse, upper_inverse):
+def any_pivots(matrix, pivots, lower_inverse, upper_inverse):
     process_row = lax.axis_index("prow")
     process_col = lax.axis_index("pcol")
     prow_count = lax.axis_size("prow")
@@ -54,6 +524,21 @@
     return current
 
 
+def spread(matrix, lower_inverse, upper_inverse, index, order, slot_hot, put):
+    rows, tops, ext = gather(matrix, index, order)
+    return finish(matrix, rows, tops, ext, put, slot_hot, lower_inverse, upper_inverse)
+
+
+def shards(matrix, pivots, lower_inverse, upper_inverse):
+    p = lax.axis_index("prow")
+    fits, index, order, slot_hot, put = plan(pivots, p)
+    return lax.cond(
+        fits,
+        lambda: spread(matrix, lower_inverse, upper_inverse, index, order, slot_hot, put),
+        lambda: any_pivots(matrix, pivots, lower_inverse, upper_inverse),
+    )
+
+
 def solution(mesh):
     placed = (P("prow", "pcol"), P(), P(), P())
     return jax.shard_map(

time: 533 us -> 124 us (0.23)
  waiting for transfers between devices: 432 us -> 0 us
  Pallas kernels: 0 us -> 83.4 us
  matrix products: 28.5 us -> 0.91 us
  other arithmetic: 29.7 us -> 10.4 us
  local copies, waits for them, and re-layouts: 25.1 us -> 10 us
  between operations: 13.3 us -> 19.2 us
    psum x4 -> x0, waiting for transfers between devices: 432 us -> none  [the longest x2 313 us: shards(): in_play = lax.psum(picked, 'prow')]
    pallas_call x0 -> x2, Pallas kernels: none -> 83.4 us  [the longest x1 72.1 us: gather(): pl.pallas_call(gather_kernel, out_shape=[jax.ShapeDtypeStruct((256, COLS)...]
    dot_general x6 -> x1, matrix products: 28.5 us -> 0.91 us  [plan(): jnp.dot(jnp.concatenate(row_hots, 1), jnp.concatenate(group_hots, 0), pre...]
    scatter x6 -> x0, other arithmetic: 24.7 us -> none  [the longest x2 16.1 us: shards(): current.at[jnp.where(owned, local_row, rows_dev)].set(arrived, mode='drop')]
    gather x2 -> x0, local copies, waits for them, and re-layouts: 12 us -> none  [shards(): picked = jnp.where(owned[:, None], current[local_row], 0.0)]
  transfers between devices with their start and end apart: 4 -> 0, of which waited for: 4 -> 0; matrix products, arithmetic and copies ran while one was open for 1% -> 0% of each run, Pallas kernels for 0% -> 0%
where the time goes in v1:
time: 124 us
  Pallas kernels  83.4 us (67%)
  between operations  19.2 us (15%)
  other arithmetic  10.4 us (8%)
  local copies, waits for them, and re-layouts  10 us (8%)
    pallas_call x1, Pallas kernels, gather(): pl.pallas_call(gather_kernel, out_shape=[jax.ShapeDtypeStruct((256, COLS)...  72.1 us
    pallas_call x1, Pallas kernels, finish(): pl.pallas_call(finish_kernel, grid=(COLS // WIDTH,), out_shape=jax.ShapeD...  11.3 us
    unnamed x9, local copies, waits for them, and re-layouts  6.7 us

profile of v1, /device:TPU:17, one launch (start us, length us, event | category | flops | bytes accessed | tf_op | source)
XLA Modules:
  0.0 123.9 jit_solution(18231068344018511337)
XLA Ops:
  6.5 6.2 %copy.30 = f32[512,3072]{1,0:T(8,128)} copy(f32[512,3072]{1,0:T(8,128)} %param.14) | data formatting | bytes 12582912
  12.8 0.5 iota.204
  13.5 0.2 compare_reduce_fusion.2
  14.1 0.7 fusion.113
  16.1 0.7 or_reduce_fusion.1
  16.8 0.6 fusion.112
  18.7 0.7 or_reduce_fusion
  19.6 0.7 fusion.110
  21.5 1.2 compare_reduce_fusion.4
  24.8 0.5 copy-done.7
  25.5 0.9 fusion.68
  26.4 0.6 fusion.81
  27.0 0.6 fusion.80
  27.8 0.6 broadcast.1977
  28.4 0.6 ne.841
  28.9 0.5 broadcast.1979
  29.5 87.6 %conditional.1 = (f32[512,3072]{1,0:T(8,128)}) conditional(s32[]{:T(128)} %convert_element_type.34, (s32[256]{0:T(256)S(1)}, f32[512,3072]{1,0:T(8,128)}, f32[2,128,128]{2,1,0:T(8,128)S(1)}, f32[2,128,128]{2,1,0:T(8,128)}) %tuple.91, (s32[256]{0:T(256)}, s32[1,256]{1,0:T(1,128)}, s32[]{:T(128)}, s32[]{:T(128)}, pred[1,256]{1,0:T(4,128)(4,1)S(1)}, ...), branch_computations={%region_17.25_spmd, %region_25.27_spmd} | conditional | flops 6257055744 | bytes 147655552 | solution.py:535
  29.5 0.7 and_select_fusion.15
  30.2 0.7 compare_reduce_fusion.1
  30.9 0.6 fusion.66
  31.7 0.9 broadcast_select_fusion.2.order_ref
  32.6 1.1 copy.8.put_ref
  33.7 72.1 %gather_rows.1 = (f32[256,3072]{1,0:T(8,128)S(1)}, f32[88,3072]{1,0:T(8,128)S(1)}, f32[2,856,128]{2,1,0:T(8,128)S(1)}) custom-call(s32[56]{0:T(128)S(1)} %broadcast_add_fusion.index_ref, f32[128,128]{1,0:T(8,128)S(1)} %broadcast_select_fusion.2.order_ref, f32[512,3072]{1,0:T(8,128)} %get-tuple-element.240.a_hbm.a_ref), custom_call_target="tpu_custom_call" | custom-call | tf_op jit(solution)/shard_map/cond/branch_1_fun/gather_rows/pallas_call | solution.py:370
  105.8 11.3 %finish.1 = f32[512,3072]{1,0:T(8,128)} custom-call(f32[512,3072]{1,0:T(8,128)S(1)} %copy-done, f32[256,3072]{1,0:T(8,128)S(1)} %get-tuple-element.256.r_ref, f32[88,3072]{1,0:T(8,128)S(1)} %get-tuple-element.257.t_ref, f32[2,856,128]{2,1,0:T(8,128)S(1)} %get-tuple-element.258.e_ref, f32[512,88]{1,0:T(8,128)S(1)} %copy.8.put_ref, ...), custom_call_target="tpu_custom_call" | custom-call | tf_op jit(solution)/shard_map/cond/branch_1_fun/finish/pallas_call | solution.py:460
  (35 shorter events, 1.5 us)
Async XLA Ops:
  6.5 6.7 %copy-start.6 = (s32[256]{0:T(256)S(1)}, s32[256]{0:T(256)}, u32[]{:S(2)}) copy-start(s32[256]{0:T(256)} %param.15) | copy-start | bytes 3076
  6.5 22.9 %copy-start.3 = (f32[2,128,128]{2,1,0:T(8,128)S(1)}, f32[2,128,128]{2,1,0:T(8,128)}, u32[]{:S(2)}) copy-start(f32[2,128,128]{2,1,0:T(8,128)} %param.17) | copy-start | bytes 393220
  24.7 0.6 copy-start.7
  24.7 0.6 copy-start.8
  32.6 73.2 %copy-start.5 = (f32[2,128,128]{2,1,0:T(8,128)S(1)}, f32[2,128,128]{2,1,0:T(8,128)}, u32[]{:S(2)}) copy-start(f32[2,128,128]{2,1,0:T(8,128)} %get-tuple-element.261.low_ref) | copy-start | bytes 393220 | tf_op jit(solution)/shard_map/cond
  33.7 72.1 %copy-start = (f32[512,3072]{1,0:T(8,128)S(1)}, f32[512,3072]{1,0:T(8,128)}, u32[]{:S(2)}) copy-start(f32[512,3072]{1,0:T(8,128)} %get-tuple-element.240.a_hbm.a_ref) | copy-start | bytes 18874372 | tf_op jit(solution)/shard_map/cond

commit v2 on v1

v2 whole, which is shorter than its diff:
```python
import functools

import jax
import jax.numpy as jnp
from jax import lax
from jax.experimental import pallas as pl
from jax.experimental.pallas import tpu as pltpu
from jax.sharding import PartitionSpec as P

MESH = pl.DeviceIdType.MESH
NB = 128
ROWS = 512
COLS = 3072
NPROW = 32
REACH_R = 3
REACH_T = 5
GROUPS_R = 2 * REACH_R + 1
GROUPS_T = 2 * REACH_T + 1
TROWS = 8 * GROUPS_T
EXT = ROWS + 256 + TROWS
F32 = jnp.float32
BF16 = jnp.bfloat16
I32 = jnp.int32


def hp(a, b):
    return jnp.dot(a, b, precision=lax.Precision.HIGHEST, preferred_element_type=F32)


def hot(mask):
    return jnp.where(mask, 1.0, 0.0).astype(F32)


def owner_of(row):
    return (row >> 7) & (NPROW - 1)


def local_of(row):
    return ((row >> 12) << 7) + (row & (NB - 1))


def wrapped(distance):
    return ((distance + 16) & (NPROW - 1)) - 16


def iota(shape, dim):
    return lax.broadcasted_iota(I32, shape, dim)


def both(row):
    n = row.shape[1]
    eye = iota((n, n), 0) == iota((n, n), 1)
    return row, jnp.sum(jnp.where(eye, row, 0), axis=1, keepdims=True)


def ranked(row, col):
    n = row.shape[1]
    key_row, key_col = row * n + iota((1, n), 1), col * n + iota((n, 1), 0)
    in_row = jnp.sum(jnp.where(key_col < key_row, 1, 0), axis=0, keepdims=True)
    in_col = jnp.sum(jnp.where(key_row < key_col, 1, 0), axis=1, keepdims=True)
    return in_row, in_col


def plan_kernel(piv_ref, fits_ref, meta_ref, index_ref, order_ref, slot_ref, put_ref):
    p = lax.axis_index("prow")
    r0, r1 = piv_ref[0:1, :], piv_ref[1:2, :]
    c0 = both(r0)[1]
    line, lane = iota((NB, NB), 0), iota((NB, NB), 1)
    same = c0 == r1
    onto = c0 - NB == lane
    same_i, onto_i = jnp.where(same, 1, 0), jnp.where(onto, 1, 0)
    src1 = jnp.where(jnp.max(same_i, axis=0, keepdims=True) > 0, jnp.sum(same_i * line, axis=0, keepdims=True), r1)
    via = jnp.sum(jnp.where(onto, r1, 0), axis=1, keepdims=True)
    dest0_col = jnp.where(c0 < 2 * NB, via, jnp.where(jnp.max(same_i, axis=1, keepdims=True) > 0, -1, c0))
    dest0 = jnp.sum(jnp.where(line == lane, dest0_col, 0), axis=0, keepdims=True)
    dest1, dest1_col = both(jnp.where(jnp.max(onto_i, axis=0, keepdims=True) > 0, -1, r1))
    meta_ref[0:1, :] = r0
    meta_ref[1:2, :] = src1
    meta_ref[2:3, :] = dest0
    meta_ref[3:4, :] = dest1
    meta_ref[4:8, :] = jnp.zeros((4, NB), I32)

    src, src_col = jnp.concatenate([r0, src1], 1), jnp.concatenate([c0, both(src1)[1]], 0)
    own, own_col = owner_of(src), owner_of(src_col)
    rank, rank_col = ranked(own, own_col)
    skew = 16 * own + 7 - 2 * rank
    turn = (jnp.max(skew, axis=1, keepdims=True) + jnp.min(skew, axis=1, keepdims=True)) >> 2
    slot, slot_col = (rank + turn) & 255, (rank_col + turn) & 255
    off_r = jnp.max(jnp.abs(wrapped((slot >> 3) - own)))
    wanted = (8 * (p - REACH_R) + iota((1, NB), 1)) & 255
    mine = (slot_col == wanted) & (own_col == p)
    index_ref[0:1, :] = jnp.sum(jnp.where(mine, local_of(src_col) + 1, 0), axis=0, keepdims=True) - 1
    slot_ref[...] = hot(slot_col == iota((256, 256), 1))

    put = jnp.zeros((ROWS, NB), F32)
    off_t = 0
    for section, (dest, dest_col) in enumerate(((dest0, dest0_col), (dest1, dest1_col))):
        to = jnp.where(dest >= 0, owner_of(dest), iota((1, NB), 1) >> 2)
        to_col = jnp.where(dest_col >= 0, owner_of(dest_col), iota((NB, 1), 0) >> 2)
        rank, rank_col = ranked(to, to_col)
        skew = 8 * to + 3 - 2 * rank
        turn = (jnp.max(skew, axis=1, keepdims=True) + jnp.min(skew, axis=1, keepdims=True)) >> 2
        place, place_col = (rank + turn) & (NB - 1), (rank_col + turn) & (NB - 1)
        home, home_col = (
            (v >> 4) * 4 + jnp.where(((v >> 3) & 1) == 0, section, 3 - section) for v in (place, place_col)
        )
        off_t = jnp.maximum(off_t, jnp.max(jnp.where(dest >= 0, jnp.abs(wrapped(to - home)), 0)))
        column = ((home_col - p + REACH_T) & (NPROW - 1)) * 8 + (place_col & 7)
        here = (dest >= 0) & (to == p)
        into = hot((local_of(dest) == iota((ROWS, NB), 0)) & here)
        put = put + jnp.dot(into, hot(column == lane), preferred_element_type=F32)

        @pl.when((p == section) | (section == 1) & (p > 1))
        def _():
            order_ref[...] = hot(place == line)

    put_ref[...] = put[:, :TROWS]
    fits_ref[0] = jnp.where((off_r <= REACH_R) & (off_t <= REACH_T), 1, 0)


def plan(pivots):
    vmem = pl.BlockSpec(memory_space=pltpu.VMEM)
    return pl.pallas_call(
        plan_kernel,
        out_shape=[
            jax.ShapeDtypeStruct((1,), I32),
            jax.ShapeDtypeStruct((8, NB), I32),
            jax.ShapeDtypeStruct((1, NB), I32),
            jax.ShapeDtypeStruct((NB, NB), F32),
            jax.ShapeDtypeStruct((256, 256), F32),
            jax.ShapeDtypeStruct((ROWS, TROWS), F32),
        ],
        in_specs=[vmem],
        out_specs=[pl.BlockSpec(memory_space=pltpu.SMEM), vmem, vmem, vmem, vmem, vmem],
        name="plan",
    )(pivots.reshape(2, NB))


A_CHUNKS = ((0, 128, 1), (128, 512, -1), (640, 640, 1))
B_CHUNKS = ((1280, 896, 1), (2176, 896, -1))
SHIFTS = ((0, 128), (1280, 1792), (128, 1152))
T_CHUNKS = ((0, 128), (128, 2944))
COPIES = 224


def hops(long, way):
    return 4 if long == way else 3


def gather_kernel(
    index_ref, order_ref, slot_ref, put_ref, low_ref, up_ref, a_hbm,
    r_ref, t_ref, w_ref, put16_ref, keep_ref, first_ref,
    a_ref, pack, inbox, t_pack, e_ref, load_sem, send_sem, recv_sem,
):
    p, q = lax.axis_index("prow"), lax.axis_index("pcol")
    z, x = lax.div(p, 4), lax.rem(p, 4)
    y, core = lax.div(q, 2), lax.rem(q, 2)
    source = p < 2
    sends, receipts = {}, {}
    pending = []

    def number(numbers, tag):
        assert len(numbers) < COPIES or tag in numbers
        return numbers.setdefault(tag, len(numbers))

    def copy(src, dst, tag, device, recv_tag=None):
        return pltpu.make_async_remote_copy(
            src_ref=src,
            dst_ref=dst,
            send_sem=send_sem.at[number(sends, tag)],
            recv_sem=recv_sem.at[number(receipts, recv_tag or tag)],
            device_id=device,
            device_id_type=MESH,
        )

    def send(src, dst, tag, device):
        c = copy(src, dst, tag, device)
        c.start()
        pending.append(c)

    def arrived(dst, tag):
        copy(dst, dst, tag, core_peer).wait_recv()

    def along(step):
        return lax.rem(p + step + NPROW, NPROW), q

    def at_z(step):
        return lax.rem(z + step + 8, 8) * 4 + x, q

    def at_x(step):
        return z * 4 + lax.rem(x + step + 4, 4), q

    core_peer = (p, y * 2 + 1 - core)

    def block(zz, xx, cols):
        start = pl.multiple_of((lax.rem(z + zz + 8, 8) * 4 + lax.rem(x + xx + 4, 4)) * 8, 8)
        return r_ref.at[pl.ds(start, 8), pl.ds(cols[0], cols[1])]

    def plane(zz, cols):
        start = pl.multiple_of(lax.rem(z + zz + 8, 8) * 32, 32)
        return r_ref.at[pl.ds(start, 32), pl.ds(cols[0], cols[1])]

    load = pltpu.make_async_copy(a_hbm, a_ref, load_sem.at[0])
    load.start()

    barrier = pltpu.get_barrier_semaphore()

    def greet(device):
        pl.semaphore_signal(barrier, inc=1, device_id=device, device_id_type=MESH)

    for step in range(-REACH_T, REACH_T + 1):
        if step:
            greet(along(step))
    greet(core_peer)

    @pl.when(y > 0)
    def _():
        greet((p, core))

    from_row = jnp.where((x == 0) | (x == 3), 0, 1)

    @pl.when(p != from_row)
    def _():
        greet((from_row, q))

    load.wait()

    def take(m, carry):
        r = index_ref[0, m]
        row = a_ref[pl.ds(jnp.maximum(r, 0), 1), :]
        pack[pl.ds(m, 1), :] = jnp.where(r >= 0, row, 0.0)
        return carry

    lax.fori_loop(0, 8 * GROUPS_R, take, 0)
    pl.semaphore_wait(barrier, 2 * REACH_T + 1 + jnp.where(y == 0, 3, 0) + jnp.where(source, 15, 0))

    def shift(cols):
        at = pl.ds(*cols)
        for d in range(-REACH_R, REACH_R + 1):
            if d:
                send(pack.at[pl.ds(8 * (d + REACH_R), 8), at], inbox.at[pl.ds(8 * (REACH_R - d), 8), at], ("shift", cols, d), along(d))

    def settle(cols):
        at = pl.ds(*cols)
        for d in range(-REACH_R, REACH_R + 1):
            if d:
                arrived(inbox.at[pl.ds(8 * (REACH_R - d), 8), at], ("shift", cols, d))
        total = pack[8 * REACH_R : 8 * REACH_R + 8, at]
        for d in range(-REACH_R, REACH_R + 1):
            if d:
                total = total + inbox[8 * (REACH_R - d) : 8 * (REACH_R - d) + 8, at]
        r_ref[pl.ds(pl.multiple_of(p * 8, 8), 8), at] = total

    ext_a = e_ref.at[core, pl.ds(0, ROWS)]
    ext_rt = e_ref.at[core, pl.ds(ROWS, EXT - ROWS)]
    far_a = e_ref.at[1 - core, pl.ds(0, ROWS)]
    far_rt = e_ref.at[1 - core, pl.ds(ROWS, EXT - ROWS)]

    shift(SHIFTS[0])

    @pl.when(y == 0)
    def _():
        e_ref[core, :ROWS] = a_ref[:, :NB]
        for step in (1, 3, 2):
            copy(ext_a, ext_a, ("ya", step), (p, step * 2 + core), ("ya",)).start()

    shift(SHIFTS[1])
    shift(SHIFTS[2])

    own_t = pl.ds(8 * REACH_T, 8)

    @pl.when(source)
    def _():
        def turn(n, carry):
            at = pl.ds(pl.multiple_of(n * 512, 512), 512)
            t_pack[:, at] = hp(order_ref[...], a_ref[:NB, at])
            return carry

        lax.fori_loop(0, COLS // 512, turn, 0)
        for cols in T_CHUNKS:
            at = pl.ds(*cols)
            for g in range(1, 16):
                to = g // 2 * 4 + (p if g % 2 == 0 else 3 - p)
                copy(t_pack.at[pl.ds(8 * g, 8), at], t_ref.at[own_t, at], ("ts", cols, g), (to, q), ("ts", cols)).start()
        t_ref[own_t, :] = t_pack[:8]

    def spread_x(cols):
        for dx in (1, 3, 2):
            send(block(0, 0, cols), block(0, 0, cols), ("a1", cols, dx), at_x(dx))

    def joined_x(cols):
        for dx in (1, 3, 2):
            arrived(block(0, -dx, cols), ("a1", cols, dx))

    def pass_plane(cols, s):
        for way in (1, -1):
            if s > 0:
                if s > hops(cols[2], way):
                    continue
                arrived(plane(-way * s, cols), ("a2", cols, way, s))
            if s < hops(cols[2], way):
                part = plane(-way * s, cols)
                send(part, part, ("a2", cols, way, s + 1), at_z(way))

    def ways_at(cols, s):
        return [0] if s == 0 else [-way * s for way in (1, -1) if s <= hops(cols[2], way)]

    def pass_block(cols, s):
        for way in (1, -1):
            if s > 0:
                if s > hops(cols[2], way):
                    continue
                arrived(block(-way * s, 0, cols), ("b1", cols, way, s))
            part = block(-way * s, 0, cols)
            if s < hops(cols[2], way):
                send(part, part, ("b1", cols, way, s + 1), at_z(way))
            if s > 0 or way == 1:
                for dx in (1, -1):
                    send(part, part, ("b2", cols, -way * s if s else 0, dx), at_x(dx))

    def relay_x(cols, s):
        for zz in ways_at(cols, s):
            for dx in (1, -1):
                arrived(block(zz, -dx, cols), ("b2", cols, zz, dx))
                if dx == cols[2]:
                    part = block(zz, -dx, cols)
                    send(part, part, ("b3", cols, zz), at_x(dx))

    def end_x(cols, s):
        for zz in ways_at(cols, s):
            arrived(block(zz, 2, cols), ("b3", cols, zz))

    def t_ready(cols):
        at = pl.ds(*cols)

        @pl.when(jnp.logical_not(source))
        def _():
            arrived(t_ref.at[own_t, at], ("ts", cols))

        for e in range(-REACH_T, REACH_T + 1):
            if e:
                send(t_ref.at[own_t, at], t_ref.at[pl.ds(8 * (REACH_T - e), 8), at], ("th", cols, e), along(e))

    def t_done(cols):
        at = pl.ds(*cols)
        for e in range(-REACH_T, REACH_T + 1):
            if e:
                arrived(t_ref.at[pl.ds(8 * (REACH_T - e), 8), at], ("th", cols, e))

    first, *rest = A_CHUNKS
    settle(SHIFTS[0])
    spread_x(first)
    settle(SHIFTS[1])
    for cols in B_CHUNKS:
        pass_block(cols, 0)
    settle(SHIFTS[2])
    for cols in rest:
        spread_x(cols)
    joined_x(first)
    pass_plane(first, 0)
    t_ready(T_CHUNKS[0])
    for cols in rest:
        joined_x(cols)
        pass_plane(cols, 0)
    for s in range(1, 5):
        pass_plane(first, s)
        for cols in B_CHUNKS:
            pass_block(cols, s)
        for cols in rest:
            pass_plane(cols, s)
        for cols in B_CHUNKS:
            relay_x(cols, s - 1)
        if s == 2:
            t_ready(T_CHUNKS[1])
    t_done(T_CHUNKS[0])

    @pl.when(y == 0)
    def _():
        e_ref[core, ROWS : ROWS + 256] = r_ref[:, :NB]
        e_ref[core, ROWS + 256 :] = t_ref[:, :NB]
        for step in (1, 3, 2):
            copy(ext_rt, ext_rt, ("yr", step), (p, step * 2 + core), ("yr",)).start()

    @pl.when(y > 0)
    def _():
        arrived(ext_a, ("ya",))

    send(ext_a, ext_a, ("ca",), core_peer)
    for cols in B_CHUNKS:
        relay_x(cols, 4)

    @pl.when(y > 0)
    def _():
        arrived(ext_rt, ("yr",))

    send(ext_rt, ext_rt, ("cr",), core_peer)
    arrived(far_a, ("ca",))
    arrived(far_rt, ("cr",))
    weigh(e_ref, put_ref, slot_ref, low_ref, up_ref, w_ref, put16_ref, keep_ref, first_ref)
    for s in range(5):
        for cols in B_CHUNKS:
            end_x(cols, s)
    t_done(T_CHUNKS[1])
    for c in pending:
        c.wait_send()

    @pl.when(y == 0)
    def _():
        for step in (1, 3, 2):
            copy(ext_a, ext_a, ("ya", step), (p, step * 2 + core), ("ya",)).wait_send()
            copy(ext_rt, ext_rt, ("yr", step), (p, step * 2 + core), ("yr",)).wait_send()

    @pl.when(source)
    def _():
        for cols in T_CHUNKS:
            at = pl.ds(*cols)
            for g in range(1, 16):
                to = g // 2 * 4 + (p if g % 2 == 0 else 3 - p)
                copy(t_pack.at[pl.ds(8 * g, 8), at], t_ref.at[own_t, at], ("ts", cols, g), (to, q), ("ts", cols)).wait_send()


def gather(matrix, index, order, slot_hot, put, lower_inverse, upper_inverse):
    vmem = pl.BlockSpec(memory_space=pltpu.VMEM)
    return pl.pallas_call(
        gather_kernel,
        out_shape=[
            jax.ShapeDtypeStruct((256, COLS), F32),
            jax.ShapeDtypeStruct((TROWS, COLS), F32),
            *weights_of(TROWS),
        ],
        in_specs=[pl.BlockSpec(memory_space=pltpu.SMEM), vmem, vmem, vmem, vmem, vmem, pl.BlockSpec(memory_space=pl.ANY)],
        out_specs=[vmem] * 6,
        scratch_shapes=[
            pltpu.VMEM((ROWS, COLS), F32),
            pltpu.VMEM((8 * GROUPS_R, COLS), F32),
            pltpu.VMEM((8 * GROUPS_R, COLS), F32),
            pltpu.VMEM((NB, COLS), F32),
            pltpu.VMEM((2, EXT, NB), F32),
            pltpu.SemaphoreType.DMA((1,)),
            pltpu.SemaphoreType.DMA((COPIES,)),
            pltpu.SemaphoreType.DMA((COPIES,)),
        ],
        compiler_params=pltpu.CompilerParams(collective_id=0, has_side_effects=True, vmem_limit_bytes=48 << 20),
        name="gather_rows",
    )(index, order, slot_hot, put, lower_inverse, upper_inverse, matrix)


def split(x):
    high = x.astype(BF16)
    return high, (x - high.astype(F32)).astype(BF16)


def weigh(e_ref, put_ref, slot_ref, low_ref, up_ref, w_ref, put16_ref, keep_ref, first_ref):
    p, q = lax.axis_index("prow"), lax.axis_index("pcol")
    row, col = iota((NB, NB), 0), iota((NB, NB), 1)
    lower = [jnp.where(row > col, low_ref[t], jnp.where(row == col, 1.0, 0.0)) for t in range(2)]
    upper = [jnp.where(row <= col, up_ref[t], 0.0) for t in range(2)]
    put = put_ref[...]
    top = iota((ROWS, 1), 0) < NB
    at0, at1 = top & (p == 0), top & (p == 1)
    keep = jnp.where(at0 | at1, 0.0, 1.0 - jnp.sum(put, axis=1, keepdims=True))
    keep_ref[...] = jnp.broadcast_to(keep, (ROWS, NB))
    put16_ref[...] = put.astype(BF16)
    pi0, pi1 = slot_ref[:NB], slot_ref[NB:]
    g0, g1 = hp(lower[0], pi0), hp(lower[1], pi1)
    r0, r1 = e_ref[0, ROWS : ROWS + 256], e_ref[1, ROWS : ROWS + 256]
    k0 = hp(r0, upper[0])
    m1 = g1 - hp(hp(g1, k0), g0)
    u01 = hp(g0, r1)
    c0 = keep * e_ref[0, :ROWS] + hp(put, e_ref[0, ROWS + 256 :])
    c1 = keep * e_ref[1, :ROWS] + hp(put, e_ref[1, ROWS + 256 :])
    pis = jnp.where(p == 0, pi0, pi1)
    blank = jnp.zeros((ROWS - NB, NB), F32)
    c0 = jnp.where(at0 | at1, jnp.concatenate([hp(pis, r0), blank], 0), c0)
    c1 = jnp.where(at1, jnp.concatenate([hp(pi1, r1), blank], 0), c1)
    panel0 = hp(c0, upper[0])
    middle = c1 - hp(panel0, u01)
    panel1 = hp(middle, upper[1])
    w = hp(panel0, g0) + hp(panel1, m1)
    blank2 = jnp.zeros((ROWS - NB, 256), F32)
    w = jnp.where(at0 | at1, jnp.concatenate([-jnp.where(p == 0, g0, m1), blank2], 0), w)
    high, low = split(-w)
    w_ref[:, :256] = high
    w_ref[:, 256:512] = high
    w_ref[:, 512:] = low
    u01_tall = jnp.concatenate([u01, blank], 0)
    first0 = jnp.where(at0, c0, panel0)
    first1 = jnp.where(at0, u01_tall, jnp.where(at1, middle, panel1))
    first_ref[...] = jnp.where(q == 0, first0, first1)


def weights_of(trows):
    return [
        jax.ShapeDtypeStruct((ROWS, 768), BF16),
        jax.ShapeDtypeStruct((ROWS, trows), BF16),
        jax.ShapeDtypeStruct((ROWS, NB), F32),
        jax.ShapeDtypeStruct((ROWS, NB), F32),
    ]


WIDTH = 512


def finish_kernel(a_ref, r_ref, t_ref, w_ref, put16_ref, keep_ref, first_ref, o_ref):
    r_high, r_low = split(r_ref[...])
    t_high, t_low = split(t_ref[...])
    dot = functools.partial(jnp.dot, preferred_element_type=F32)
    rows = jnp.concatenate([r_high, r_low, r_high], 0)
    put16 = put16_ref[...]
    moved = dot(put16, t_high) + dot(put16, t_low)
    o_ref[...] = keep_ref[:, :1] * a_ref[...] + (moved + dot(w_ref[...], rows))

    @pl.when((pl.program_id(0) == 0) & (lax.axis_index("pcol") < 2))
    def _():
        o_ref[:, :NB] = first_ref[...]


def finish(matrix, rows, tops, weights):
    trows = tops.shape[0]
    whole = lambda *dims: pl.BlockSpec(dims, lambda i: (0,) * len(dims))
    wide = lambda n: pl.BlockSpec((n, WIDTH), lambda i: (0, i))
    return pl.pallas_call(
        finish_kernel,
        grid=(COLS // WIDTH,),
        out_shape=jax.ShapeDtypeStruct((ROWS, COLS), F32),
        in_specs=[wide(ROWS), wide(256), wide(trows), whole(ROWS, 768), whole(ROWS, trows), whole(ROWS, NB), whole(ROWS, NB)],
        out_specs=wide(ROWS),
        compiler_params=pltpu.CompilerParams(vmem_limit_bytes=48 << 20),
        name=f"finish_{trows}",
    )(matrix, rows, tops, *weights)


def any_pivots(matrix, meta, slot_hot, lower_inverse, upper_inverse):
    p, q = lax.axis_index("prow"), lax.axis_index("pcol")
    src, dest = meta[:2].reshape(256), meta[2:4].reshape(256)
    lines = jnp.arange(ROWS, dtype=I32)
    mine = hot((local_of(src)[:, None] == lines[None, :]) & (owner_of(src) == p)[:, None])
    rows = hp(hp(slot_hot.T, mine), matrix)
    section = (jnp.arange(256) // NB == p)[:, None]
    tops = jnp.where(section, jnp.concatenate([matrix[:NB], matrix[:NB]], 0), 0.0)
    rows, tops = lax.psum((rows, tops), "prow")
    here = (dest >= 0) & (owner_of(dest) == p)
    put = hot((local_of(dest)[None, :] == lines[:, None]) & here[None, :])
    held = jnp.concatenate([matrix[:, :NB], rows[:, :NB], tops[:, :NB]], 0)
    ext = jnp.stack([lax.psum(jnp.where(q == k, held, 0.0), "pcol") for k in range(2)])
    weights = pl.pallas_call(
        weigh,
        out_shape=weights_of(256),
        compiler_params=pltpu.CompilerParams(vmem_limit_bytes=48 << 20),
        name="weigh",
    )(ext, put, slot_hot, lower_inverse, upper_inverse)
    return finish(matrix, rows, tops, weights)


def spread_pivots(matrix, index, order, slot_hot, put, lower_inverse, upper_inverse):
    rows, tops, *weights = gather(matrix, index, order, slot_hot, put, lower_inverse, upper_inverse)
    return finish(matrix, rows, tops, weights)


def shards(matrix, pivots, lower_inverse, upper_inverse):
    fits, meta, index, order, slot_hot, put = plan(pivots)
    return lax.cond(
        fits[0] > 0,
        lambda: spread_pivots(matrix, index, order, slot_hot, put, lower_inverse, upper_inverse),
        lambda: any_pivots(matrix, meta, slot_hot, lower_inverse, upper_inverse),
    )


def solution(mesh):
    placed = (P("prow", "pcol"), P(), P(), P())
    return jax.shard_map(
        shards, mesh=mesh, in_specs=placed, out_specs=P("prow", "pcol"), check_vma=False
    )
```

time: 124 us -> 101 us (0.81)
  other arithmetic: 10.4 us -> 0 us
  local copies, waits for them, and re-layouts: 10 us -> 0.01 us
  between operations: 19.2 us -> 14 us
  Pallas kernels: 83.4 us -> 86.8 us
    unnamed x9 -> x0, local copies, waits for them, and re-layouts: 6.7 us -> none
    pallas_call x1, Pallas kernels: 72.1 us -> 77.4 us  [gather(): pl.pallas_call(gather_kernel, out_shape=[jax.ShapeDtypeStruct((256, COLS)...]
    pallas_call x1, Pallas kernels: 11.3 us -> 6.8 us  [finish(): pl.pallas_call(finish_kernel, grid=(COLS // WIDTH,), out_shape=jax.ShapeD...]
    pallas_call x0 -> x1, Pallas kernels: none -> 2.69 us  [plan(): pl.pallas_call(plan_kernel, out_shape=[jax.ShapeDtypeStruct((1,), I32), j...]
    reduce_and x3 -> x0, other arithmetic: 2.59 us -> none  [the longest x2 1.38 us: plan(): fits = fits & jnp.all((jnp.abs(wrapped(to - home)) <= REACH_T) | ~moves)]
    another operation x3 -> x0, local copies, waits for them, and re-layouts: 2.21 us -> none
    reduce_min x3 -> x0, other arithmetic: 1.96 us -> none  [the longest x2 1.3 us: plan(): place = (rank + (jnp.max(skew) + jnp.min(skew)) // 4) % NB]
    select_n x3 -> x0, other arithmetic: 1.58 us -> none  [the longest x1 0.86 us: plan(): order = jnp.where(p == 0, orders[0], orders[1])]
where the time goes in v2:
time: 101 us
  Pallas kernels  86.8 us (86%)
  between operations  14 us (14%)
    pallas_call x1, Pallas kernels, gather(): pl.pallas_call(gather_kernel, out_shape=[jax.ShapeDtypeStruct((256, COLS)...  77.4 us
    pallas_call x1, Pallas kernels, finish(): pl.pallas_call(finish_kernel, grid=(COLS // WIDTH,), out_shape=jax.ShapeD...  6.8 us
    pallas_call x1, Pallas kernels, plan(): pl.pallas_call(plan_kernel, out_shape=[jax.ShapeDtypeStruct((1,), I32), j...  2.69 us

profile of v2, /device:TPU:17, one launch (start us, length us, event | category | flops | bytes accessed | tf_op | source)
XLA Modules:
  0.0 100.9 jit_solution(11788894279855237787)
XLA Ops:
  6.5 2.7 %plan.1 = (s32[1]{0:T(128)}, s32[8,128]{1,0:T(8,128)S(1)}, s32[1,128]{1,0:T(1,128)S(1)}, f32[128,128]{1,0:T(8,128)}, f32[256,256]{1,0:T(8,128)S(1)}, /*index=5*/f32[512,88]{1,0:T(8,128)}) custom-call(s32[2,128]{1,0:T(2,128)} %bitcast.17), custom_call_target="tpu_custom_call" | custom-call | tf_op jit(solution)/shard_map/plan/pallas_call | solution.py:123
  9.9 84.2 %conditional.1 = (f32[512,3072]{1,0:T(8,128)}) conditional(s32[]{:T(128)} %bitcast.7, (s32[8,128]{1,0:T(8,128)S(1)}, f32[256,256]{1,0:T(8,128)S(1)}, f32[512,3072]{1,0:T(8,128)}, f32[2,128,128]{2,1,0:T(8,128)}, f32[2,128,128]{2,1,0:T(8,128)}) %tuple.11, (s32[1,128]{1,0:T(1,128)S(1)}, f32[128,128]{1,0:T(8,128)}, f32[256,256]{1,0:T(8,128)S(1)}, ...), branch_computations={%region_0.5_spmd, %region_5.6_spmd} | conditional | flops 5239478272 | bytes 83109632 | solution.py:562
  9.9 0.0 copy-start.2
  9.9 77.4 %gather_rows.1 = (f32[256,3072]{1,0:T(8,128)S(1)}, f32[88,3072]{1,0:T(8,128)S(1)}, bf16[512,768]{1,0:T(8,128)(2,1)S(1)}, bf16[512,88]{1,0:T(8,128)(2,1)S(1)}, f3...) custom-call(s32[1,128]{1,0:T(1,128)S(1)} %get-tuple-element.42.index_ref, f32[128,128]{1,0:T(8,128)} %get-tuple-element.43.order_ref, ...), custom_call_target="tpu_custom_call" | custom-call | tf_op jit(solution)/shard_map/cond/branch_1_fun/gather_rows/pallas_call | solution.py:424
  87.3 0.0 copy-done.2
  87.3 6.8 %finish_88.1 = f32[512,3072]{1,0:T(8,128)} custom-call(f32[512,3072]{1,0:T(8,128)S(1)} %copy-done.2, f32[256,3072]{1,0:T(8,128)S(1)} %get-tuple-element.48.r_ref, f32[88,3072]{1,0:T(8,128)S(1)} %get-tuple-element.49.t_ref, bf16[512,768]{1,0:T(8,128)(2,1)S(1)} %get-tuple-element.50.w_ref, bf16[512,88]{1,0:T(8,128)(2,1)S(1)} %get-tuple-element.51.put16_ref, ...), custom_call_target="tpu_custom_call" | custom-call | tf_op jit(solution)/shard_map/cond/branch_1_fun/finish_88/pallas_call | solution.py:522
Async XLA Ops:
  9.9 77.4 %copy-start.2 = (f32[512,3072]{1,0:T(8,128)S(1)}, f32[512,3072]{1,0:T(8,128)}, u32[]{:S(2)}) copy-start(f32[512,3072]{1,0:T(8,128)} %get-tuple-element.41.a_hbm.a_ref) | copy-start | bytes 18874372 | tf_op jit(solution)/shard_map/cond

commit v3 on v2

--- a/solution.py
+++ b/solution.py
@@ -370,7 +370,7 @@
             pass_plane(cols, s)
         for cols in B_CHUNKS:
             relay_x(cols, s - 1)
-        if s == 2:
+        if s == 4:
             t_ready(T_CHUNKS[1])
     t_done(T_CHUNKS[0])
 

time: 101 us -> 90.2 us (0.89)
  Pallas kernels: 86.8 us -> 76 us
    pallas_call x1, Pallas kernels: 77.4 us -> 66.5 us  [gather(): pl.pallas_call(gather_kernel, out_shape=[jax.ShapeDtypeStruct((256, COLS)...]
where the time goes in v3:
time: 90.2 us; the launch traced here: 90.1 us
  Pallas kernels  76 us (84%)
  between operations  14 us (16%)
    pallas_call x1, Pallas kernels, gather(): pl.pallas_call(gather_kernel, out_shape=[jax.ShapeDtypeStruct((256, COLS)...  66.5 us
    pallas_call x1, Pallas kernels, finish(): pl.pallas_call(finish_kernel, grid=(COLS // WIDTH,), out_shape=jax.ShapeD...  6.8 us
    pallas_call x1, Pallas kernels, plan(): pl.pallas_call(plan_kernel, out_shape=[jax.ShapeDtypeStruct((1,), I32), j...  2.69 us

profile of v3, /device:TPU:17, one launch (start us, length us, event | category | flops | bytes accessed | tf_op | source)
XLA Modules:
  0.0 90.1 jit_solution(8353245948808178421)
XLA Ops:
  6.5 2.7 %plan.1 = (s32[1]{0:T(128)}, s32[8,128]{1,0:T(8,128)S(1)}, s32[1,128]{1,0:T(1,128)S(1)}, f32[128,128]{1,0:T(8,128)}, f32[256,256]{1,0:T(8,128)S(1)}, /*index=5*/f32[512,88]{1,0:T(8,128)}) custom-call(s32[2,128]{1,0:T(2,128)} %bitcast.17), custom_call_target="tpu_custom_call" | custom-call | tf_op jit(solution)/shard_map/plan/pallas_call | solution.py:123
  9.9 73.4 %conditional.1 = (f32[512,3072]{1,0:T(8,128)}) conditional(s32[]{:T(128)} %bitcast.7, (s32[8,128]{1,0:T(8,128)S(1)}, f32[256,256]{1,0:T(8,128)S(1)}, f32[512,3072]{1,0:T(8,128)}, f32[2,128,128]{2,1,0:T(8,128)}, f32[2,128,128]{2,1,0:T(8,128)}) %tuple.11, (s32[1,128]{1,0:T(1,128)S(1)}, f32[128,128]{1,0:T(8,128)}, f32[256,256]{1,0:T(8,128)S(1)}, ...), branch_computations={%region_0.5_spmd, %region_5.6_spmd} | conditional | flops 5239478272 | bytes 83109632 | solution.py:562
  9.9 0.0 copy-start.2
  9.9 66.5 %gather_rows.1 = (f32[256,3072]{1,0:T(8,128)S(1)}, f32[88,3072]{1,0:T(8,128)S(1)}, bf16[512,768]{1,0:T(8,128)(2,1)S(1)}, bf16[512,88]{1,0:T(8,128)(2,1)S(1)}, f3...) custom-call(s32[1,128]{1,0:T(1,128)S(1)} %get-tuple-element.42.index_ref, f32[128,128]{1,0:T(8,128)} %get-tuple-element.43.order_ref, ...), custom_call_target="tpu_custom_call" | custom-call | tf_op jit(solution)/shard_map/cond/branch_1_fun/gather_rows/pallas_call | solution.py:424
  76.5 0.0 copy-done.2
  76.5 6.8 %finish_88.1 = f32[512,3072]{1,0:T(8,128)} custom-call(f32[512,3072]{1,0:T(8,128)S(1)} %copy-done.2, f32[256,3072]{1,0:T(8,128)S(1)} %get-tuple-element.48.r_ref, f32[88,3072]{1,0:T(8,128)S(1)} %get-tuple-element.49.t_ref, bf16[512,768]{1,0:T(8,128)(2,1)S(1)} %get-tuple-element.50.w_ref, bf16[512,88]{1,0:T(8,128)(2,1)S(1)} %get-tuple-element.51.put16_ref, ...), custom_call_target="tpu_custom_call" | custom-call | tf_op jit(solution)/shard_map/cond/branch_1_fun/finish_88/pallas_call | solution.py:522
Async XLA Ops:
  9.9 66.6 %copy-start.2 = (f32[512,3072]{1,0:T(8,128)S(1)}, f32[512,3072]{1,0:T(8,128)}, u32[]{:S(2)}) copy-start(f32[512,3072]{1,0:T(8,128)} %get-tuple-element.41.a_hbm.a_ref) | copy-start | bytes 18874372 | tf_op jit(solution)/shard_map/cond

commit v4 on v3

--- a/solution.py
+++ b/solution.py
@@ -498,7 +498,7 @@
     ]
 
 
-WIDTH = 512
+WIDTH = 768
 
 
 def finish_kernel(a_ref, r_ref, t_ref, w_ref, put16_ref, keep_ref, first_ref, o_ref):

time: 90.2 us -> 90.3 us (level)
  no operation moved by 1% of the time
where the time goes in v4:
time: 90.3 us; the launch traced here: 90.2 us
  Pallas kernels  76.1 us (84%)
  between operations  14 us (16%)
    pallas_call x1, Pallas kernels, gather(): pl.pallas_call(gather_kernel, out_shape=[jax.ShapeDtypeStruct((256, COLS)...  66.8 us
    pallas_call x1, Pallas kernels, finish(): pl.pallas_call(finish_kernel, grid=(COLS // WIDTH,), out_shape=jax.ShapeD...  6.62 us
    pallas_call x1, Pallas kernels, plan(): pl.pallas_call(plan_kernel, out_shape=[jax.ShapeDtypeStruct((1,), I32), j...  2.69 us

profile of v4, /device:TPU:17, one launch (start us, length us, event | category | flops | bytes accessed | tf_op | source)
XLA Modules:
  0.0 90.2 jit_solution(12637362760377834239)
XLA Ops:
  6.5 2.7 %plan.1 = (s32[1]{0:T(128)}, s32[8,128]{1,0:T(8,128)S(1)}, s32[1,128]{1,0:T(1,128)S(1)}, f32[128,128]{1,0:T(8,128)}, f32[256,256]{1,0:T(8,128)S(1)}, /*index=5*/f32[512,88]{1,0:T(8,128)}) custom-call(s32[2,128]{1,0:T(2,128)} %bitcast.17), custom_call_target="tpu_custom_call" | custom-call | tf_op jit(solution)/shard_map/plan/pallas_call | solution.py:123
  9.9 73.5 %conditional.1 = (f32[512,3072]{1,0:T(8,128)}) conditional(s32[]{:T(128)} %bitcast.7, (s32[8,128]{1,0:T(8,128)S(1)}, f32[256,256]{1,0:T(8,128)S(1)}, f32[512,3072]{1,0:T(8,128)}, f32[2,128,128]{2,1,0:T(8,128)}, f32[2,128,128]{2,1,0:T(8,128)}) %tuple.11, (s32[1,128]{1,0:T(1,128)S(1)}, f32[128,128]{1,0:T(8,128)}, f32[256,256]{1,0:T(8,128)S(1)}, ...), branch_computations={%region_0.5_spmd, %region_5.6_spmd} | conditional | flops 5239478272 | bytes 83109632 | solution.py:562
  9.9 0.0 copy-start.2
  9.9 66.8 %gather_rows.1 = (f32[256,3072]{1,0:T(8,128)S(1)}, f32[88,3072]{1,0:T(8,128)S(1)}, bf16[512,768]{1,0:T(8,128)(2,1)S(1)}, bf16[512,88]{1,0:T(8,128)(2,1)S(1)}, f3...) custom-call(s32[1,128]{1,0:T(1,128)S(1)} %get-tuple-element.42.index_ref, f32[128,128]{1,0:T(8,128)} %get-tuple-element.43.order_ref, ...), custom_call_target="tpu_custom_call" | custom-call | tf_op jit(solution)/shard_map/cond/branch_1_fun/gather_rows/pallas_call | solution.py:424
  76.7 0.0 copy-done.2
  76.7 6.6 %finish_88.1 = f32[512,3072]{1,0:T(8,128)} custom-call(f32[512,3072]{1,0:T(8,128)S(1)} %copy-done.2, f32[256,3072]{1,0:T(8,128)S(1)} %get-tuple-element.48.r_ref, f32[88,3072]{1,0:T(8,128)S(1)} %get-tuple-element.49.t_ref, bf16[512,768]{1,0:T(8,128)(2,1)S(1)} %get-tuple-element.50.w_ref, bf16[512,88]{1,0:T(8,128)(2,1)S(1)} %get-tuple-element.51.put16_ref, ...), custom_call_target="tpu_custom_call" | custom-call | tf_op jit(solution)/shard_map/cond/branch_1_fun/finish_88/pallas_call | solution.py:522
Async XLA Ops:
  9.9 66.8 %copy-start.2 = (f32[512,3072]{1,0:T(8,128)S(1)}, f32[512,3072]{1,0:T(8,128)}, u32[]{:S(2)}) copy-start(f32[512,3072]{1,0:T(8,128)} %get-tuple-element.41.a_hbm.a_ref) | copy-start | bytes 18874372 | tf_op jit(solution)/shard_map/cond

commit v5 on v3

--- a/solution.py
+++ b/solution.py
@@ -140,7 +140,10 @@
 B_CHUNKS = ((1280, 896, 1), (2176, 896, -1))
 SHIFTS = ((0, 128), (1280, 1792), (128, 1152))
 T_CHUNKS = ((0, 128), (128, 2944))
-COPIES = 224
+COPIES = 240
+TOPS_AT = (4, 4)
+PREPACK = True
+GROUP_ORDER = tuple(range(1, 16))
 
 
 def hops(long, way):
@@ -232,6 +235,29 @@
         return carry
 
     lax.fori_loop(0, 8 * GROUPS_R, take, 0)
+
+    def turn_all():
+        order16 = order_ref[...].astype(BF16)
+
+        def turn(n, carry):
+            at = pl.ds(pl.multiple_of(n * 512, 512), 512)
+            rows = a_ref[:NB, at]
+            high = rows.astype(BF16)
+            rest = rows - high.astype(F32)
+            middle = rest.astype(BF16)
+            low = (rest - middle.astype(F32)).astype(BF16)
+            dot = functools.partial(jnp.dot, preferred_element_type=F32)
+            t_pack[:, at] = dot(order16, high) + (dot(order16, middle) + dot(order16, low))
+            return carry
+
+        lax.fori_loop(0, COLS // 512, turn, 0)
+
+    if PREPACK:
+
+        @pl.when(source)
+        def _():
+            turn_all()
+
     pl.semaphore_wait(barrier, 2 * REACH_T + 1 + jnp.where(y == 0, 3, 0) + jnp.where(source, 15, 0))
 
     def shift(cols):
@@ -271,15 +297,11 @@
 
     @pl.when(source)
     def _():
-        def turn(n, carry):
-            at = pl.ds(pl.multiple_of(n * 512, 512), 512)
-            t_pack[:, at] = hp(order_ref[...], a_ref[:NB, at])
-            return carry
-
-        lax.fori_loop(0, COLS // 512, turn, 0)
+        if not PREPACK:
+            turn_all()
         for cols in T_CHUNKS:
             at = pl.ds(*cols)
-            for g in range(1, 16):
+            for g in GROUP_ORDER:
                 to = g // 2 * 4 + (p if g % 2 == 0 else 3 - p)
                 copy(t_pack.at[pl.ds(8 * g, 8), at], t_ref.at[own_t, at], ("ts", cols, g), (to, q), ("ts", cols)).start()
         t_ref[own_t, :] = t_pack[:8]
@@ -346,6 +368,11 @@
         for e in range(-REACH_T, REACH_T + 1):
             if e:
                 arrived(t_ref.at[pl.ds(8 * (REACH_T - e), 8), at], ("th", cols, e))
+
+    def tops(s):
+        for k, cols in enumerate(T_CHUNKS[1:]):
+            if s == TOPS_AT[k]:
+                t_ready(cols)
 
     first, *rest = A_CHUNKS
     settle(SHIFTS[0])
@@ -370,8 +397,7 @@
             pass_plane(cols, s)
         for cols in B_CHUNKS:
             relay_x(cols, s - 1)
-        if s == 4:
-            t_ready(T_CHUNKS[1])
+        tops(s)
     t_done(T_CHUNKS[0])
 
     @pl.when(y == 0)
@@ -388,19 +414,22 @@
     send(ext_a, ext_a, ("ca",), core_peer)
     for cols in B_CHUNKS:
         relay_x(cols, 4)
+    tops(5)
 
     @pl.when(y > 0)
     def _():
         arrived(ext_rt, ("yr",))
 
     send(ext_rt, ext_rt, ("cr",), core_peer)
+    tops(6)
     arrived(far_a, ("ca",))
     arrived(far_rt, ("cr",))
     weigh(e_ref, put_ref, slot_ref, low_ref, up_ref, w_ref, put16_ref, keep_ref, first_ref)
     for s in range(5):
         for cols in B_CHUNKS:
             end_x(cols, s)
-    t_done(T_CHUNKS[1])
+    for cols in T_CHUNKS[1:]:
+        t_done(cols)
     for c in pending:
         c.wait_send()
 
@@ -414,7 +443,7 @@
     def _():
         for cols in T_CHUNKS:
             at = pl.ds(*cols)
-            for g in range(1, 16):
+            for g in GROUP_ORDER:
                 to = g // 2 * 4 + (p if g % 2 == 0 else 3 - p)
                 copy(t_pack.at[pl.ds(8 * g, 8), at], t_ref.at[own_t, at], ("ts", cols, g), (to, q), ("ts", cols)).wait_send()
 

time: 90.2 us -> 90.8 us (level)
  no operation moved by 1% of the time
where the time goes in v5:
time: 90.8 us; the launch traced here: 90.7 us
  Pallas kernels  76.6 us (84%)
  between operations  14 us (15%)
    pallas_call x1, Pallas kernels, gather(): pl.pallas_call(gather_kernel, out_shape=[jax.ShapeDtypeStruct((256, COLS)...  67.1 us
    pallas_call x1, Pallas kernels, finish(): pl.pallas_call(finish_kernel, grid=(COLS // WIDTH,), out_shape=jax.ShapeD...  6.79 us
    pallas_call x1, Pallas kernels, plan(): pl.pallas_call(plan_kernel, out_shape=[jax.ShapeDtypeStruct((1,), I32), j...  2.69 us

profile of v5, /device:TPU:17, one launch (start us, length us, event | category | flops | bytes accessed | tf_op | source)
XLA Modules:
  0.0 90.7 jit_solution(15548548692246150901)
XLA Ops:
  6.5 2.7 %plan.1 = (s32[1]{0:T(128)}, s32[8,128]{1,0:T(8,128)S(1)}, s32[1,128]{1,0:T(1,128)S(1)}, f32[128,128]{1,0:T(8,128)}, f32[256,256]{1,0:T(8,128)S(1)}, /*index=5*/f32[512,88]{1,0:T(8,128)}) custom-call(s32[2,128]{1,0:T(2,128)} %bitcast.17), custom_call_target="tpu_custom_call" | custom-call | tf_op jit(solution)/shard_map/plan/pallas_call | solution.py:123
  9.9 74.0 %conditional.1 = (f32[512,3072]{1,0:T(8,128)}) conditional(s32[]{:T(128)} %bitcast.7, (s32[8,128]{1,0:T(8,128)S(1)}, f32[256,256]{1,0:T(8,128)S(1)}, f32[512,3072]{1,0:T(8,128)}, f32[2,128,128]{2,1,0:T(8,128)}, f32[2,128,128]{2,1,0:T(8,128)}) %tuple.11, (s32[1,128]{1,0:T(1,128)S(1)}, f32[128,128]{1,0:T(8,128)}, f32[256,256]{1,0:T(8,128)S(1)}, ...), branch_computations={%region_0.5_spmd, %region_5.6_spmd} | conditional | flops 5239478272 | bytes 83109632 | solution.py:591
  9.9 0.0 copy-start.2
  9.9 67.1 %gather_rows.1 = (f32[256,3072]{1,0:T(8,128)S(1)}, f32[88,3072]{1,0:T(8,128)S(1)}, bf16[512,768]{1,0:T(8,128)(2,1)S(1)}, bf16[512,88]{1,0:T(8,128)(2,1)S(1)}, f3...) custom-call(s32[1,128]{1,0:T(1,128)S(1)} %get-tuple-element.42.index_ref, f32[128,128]{1,0:T(8,128)} %get-tuple-element.43.order_ref, ...), custom_call_target="tpu_custom_call" | custom-call | tf_op jit(solution)/shard_map/cond/branch_1_fun/gather_rows/pallas_call | solution.py:453
  77.1 0.0 copy-done.2
  77.1 6.8 %finish_88.1 = f32[512,3072]{1,0:T(8,128)} custom-call(f32[512,3072]{1,0:T(8,128)S(1)} %copy-done.2, f32[256,3072]{1,0:T(8,128)S(1)} %get-tuple-element.48.r_ref, f32[88,3072]{1,0:T(8,128)S(1)} %get-tuple-element.49.t_ref, bf16[512,768]{1,0:T(8,128)(2,1)S(1)} %get-tuple-element.50.w_ref, bf16[512,88]{1,0:T(8,128)(2,1)S(1)} %get-tuple-element.51.put16_ref, ...), custom_call_target="tpu_custom_call" | custom-call | tf_op jit(solution)/shard_map/cond/branch_1_fun/finish_88/pallas_call | solution.py:551
Async XLA Ops:
  9.9 67.2 %copy-start.2 = (f32[512,3072]{1,0:T(8,128)S(1)}, f32[512,3072]{1,0:T(8,128)}, u32[]{:S(2)}) copy-start(f32[512,3072]{1,0:T(8,128)} %get-tuple-element.41.a_hbm.a_ref) | copy-start | bytes 18874372 | tf_op jit(solution)/shard_map/cond
